TPU v7x, 32 devices: a whole 2x2x4 slice. The times are simulated.
32 devices in a mesh: dom: 16 (over z, x, core), lag: 2 (over y).
Axes of the slice: x: 2, y: 2, z: 4, core: 2. Of those that a mesh axis runs over, the one named last changes fastest.
Arguments:
- delayed_crowd_history: bfloat16 [2, 64, 512, 128], P('lag', None, 'dom'), may hold values from -6 to 6
- predicted_crowd_array: bfloat16 [64, 512, 128], P('lag', 'dom'), may hold values from -40 to 40
- probe_target_spot: int32 [256, 256], P('dom'), may hold values from 0 to 255
- alive_probe_places: int32 [256], P('dom'), may hold values from 64 to 256, as said below
- probed_heat_levels: float32 [256, 256], P('dom'), may hold values from -6 to 6
- probe_reciprocal_spread: float32 [256, 256], P('dom'), may hold values from 0.1 to 1.6
- decay_extent_squares: int32 [256], P('dom'), may hold values from 16 to 32
Outputs:
- smoothed: bfloat16 [2, 64, 512, 128], P('lag', None, 'dom')
Inputs may be any that keep to these rules, and one draw needn't show every extreme that they name: `alive_probe_places`: live observations of a patch occupy its first slots.
All inputs are finite; a program needn't handle non-finite values.
Results may differ from a plain program's by a relative error of at most 0.0062.
Values may be sent and summed in bfloat16 or wider, within the bound.
No kernel may reach another device: no remote copies, remote signals or barrier semaphores. Data moves between devices by JAX's collectives and lax.ppermute only.
A program may use at most 64 MiB of HBM per device.

v0:
```python
import functools

import jax
import jax.numpy as jnp
from jax import lax
from jax.experimental import pallas as pl
from jax.experimental.pallas import tpu as pltpu
from jax.sharding import PartitionSpec as P

PATCH = 16
NS_STEPS = 4
RADIUS = 32
FAR = RADIUS - PATCH // 2
NEAR = FAR - PATCH

NT = (((1,), (1,)), ((), ()))
NN = (((1,), (0,)), ((), ()))
f32 = jnp.float32
bf16 = jnp.bfloat16


def mm(a, b, dims=NN):
    return lax.dot_general(a, b, dims, preferred_element_type=f32)


def split(x):
    high = x.astype(bf16)
    return high, (x - high.astype(f32)).astype(bf16)


def prepare_kernel(cols, alive_ref, spot_ref, level_ref, prec_ref, hist_ref, field_ref, lag_ref, mean_ref, flat_ref):
    patches, slots = spot_ref.shape
    patch_cols = cols // PATCH
    patch_rows = patches // patch_cols
    spot = spot_ref[...]
    row_in = spot // PATCH
    col_in = spot % PATCH
    slot_index = lax.broadcasted_iota(jnp.int32, (1, slots), 1)
    iota_row = lax.broadcasted_iota(jnp.int32, (PATCH, slots), 0)
    iota_col = lax.broadcasted_iota(jnp.int32, (cols, slots), 0)
    for a in range(patch_rows):
        total = jnp.zeros((4 * PATCH, cols), f32)
        for b in range(patch_cols):
            p = a * patch_cols + b
            prec = jnp.where(slot_index < alive_ref[p], prec_ref[p : p + 1, :], 0.0)
            level = prec * level_ref[p : p + 1, :]
            prec_high = prec.astype(bf16).astype(f32)
            level_high = level.astype(bf16).astype(f32)
            on_row = row_in[p : p + 1, :] == iota_row
            pieces = [
                jnp.where(on_row, piece, 0.0).astype(bf16)
                for piece in (prec_high, prec - prec_high, level_high, level - level_high)
            ]
            on_col = jnp.where(col_in[p : p + 1, :] + b * PATCH == iota_col, 1.0, 0.0).astype(bf16)
            total = total + mm(jnp.concatenate(pieces, 0), on_col, NT)
        rows = slice(a * PATCH, (a + 1) * PATCH)
        field_ref[0, rows, :] = total[:PATCH] + total[PATCH : 2 * PATCH]
        field_ref[1, rows, :] = total[2 * PATCH : 3 * PATCH] + total[3 * PATCH :]
    members, tile_rows, _ = hist_ref.shape
    state = hist_ref[...].astype(f32)
    mean = jnp.sum(state, axis=0) / members
    mean_ref[...] = mean
    flat_ref[...] = (state - mean[None]).reshape(members * tile_rows, cols)
    for r in range(tile_rows):
        lag_ref[r] = flat_ref[pl.ds(r, members, stride=tile_rows), :].astype(bf16)


def pack_kernel(shares, place_ref, *refs):
    parts, refs = refs[:shares], refs[shares:]
    field_ref, mine_ref, mine_field_ref, message_ref, flat_ref, held_ref = refs
    share_members, tile_rows, cols = parts[0].shape
    members = share_members * shares
    lag, group = place_ref[0], place_ref[1]
    states = [part[...].astype(f32) for part in parts]
    mean = functools.reduce(jnp.add, [jnp.sum(state, axis=0) for state in states]) / members
    for k, state in enumerate(states):
        at = pl.multiple_of(lax.rem(lag + k, shares) * (share_members * tile_rows), 8)
        flat_ref[pl.ds(at, share_members * tile_rows), :] = (state - mean[None]).reshape(-1, cols)
    weight = field_ref[0]
    held_ref[0] = weight
    held_ref[1] = field_ref[1] - mean * weight

    def row(r):
        return flat_ref[pl.ds(r, members, stride=tile_rows), :].astype(bf16)

    half = mine_ref.shape[0]
    first = pl.multiple_of(group * half, 8)
    for i in range(half):
        mine_ref[i] = row(first + i)
    mine_field_ref[0] = held_ref[0, pl.ds(first, half), :]
    mine_field_ref[1] = held_ref[1, pl.ds(first, half), :]
    near = pl.multiple_of((1 - group) * (tile_rows - NEAR), 8)
    far = tile_rows - FAR
    for i in range(NEAR):
        message_ref[i] = row(near + i)
    for i in range(FAR - NEAR):
        message_ref[NEAR + i] = row(far + i)
    for k in range(2):
        rows = jnp.concatenate([held_ref[k, pl.ds(near, NEAR), :], held_ref[k, far : far + FAR - NEAR, :]], 0)
        high, low = split(rows)
        rest = jnp.zeros((members - 2 * FAR, cols), bf16)
        message_ref[FAR + k] = jnp.concatenate([high, low, rest], 0)


def taper_plan(group, relative, patch_cols, cols, radius_ref):
    patch_row = group if relative == 0 else 1 - group
    q_row = lax.broadcasted_iota(jnp.int32, (patch_cols, cols), 0)
    col = lax.broadcasted_iota(jnp.int32, (patch_cols, cols), 1)
    radius = jnp.zeros((patch_cols, cols), f32)
    for q in range(patch_cols):
        radius = jnp.where(q_row == q, radius_ref[patch_row * patch_cols + q].astype(f32), radius)
    middle = (PATCH - 1) / 2
    col_square = jnp.square(col.astype(f32) - (q_row.astype(f32) * PATCH + middle))
    return patch_row.astype(f32) * PATCH + middle, col_square, 1.0 / jnp.square(radius)


def accumulate(total, plan, anomalies, weight, innovation, first_row):
    centre_row, col_square, inverse_square = plan
    patches, cols = col_square.shape
    lefts = []
    for i, anomaly in enumerate(anomalies):
        members = anomaly.shape[0]
        offset = (first_row + i).astype(f32) - centre_row
        taper = jnp.square(jnp.maximum(0.0, 1.0 - (offset * offset + col_square) * inverse_square))
        scale = taper * weight[i : i + 1]
        blocks = anomaly.reshape(members // PATCH, PATCH, cols)
        left = [
            (blocks * jnp.broadcast_to(scale[q : q + 1], (PATCH, cols)).astype(bf16)[None]).reshape(members, cols)
            for q in range(patches)
        ]
        tail = taper * innovation[i : i + 1]
        left.append(jnp.concatenate([tail, jnp.zeros((PATCH - patches, cols), f32)], 0).astype(bf16))
        lefts.append(jnp.concatenate(left, 0))
    return total + mm(jnp.concatenate(lefts, 1), jnp.concatenate(anomalies, 1), NT)


STEP = 8


def own_kernel(place_ref, radius_ref, mine_ref, field_ref, out_ref):
    half, members, cols = mine_ref.shape
    patch_cols = cols // PATCH
    group = place_ref[1]
    totals = [jnp.zeros(out_ref.shape[1:], f32) for _ in range(2)]
    plans = [taper_plan(group, relative, patch_cols, cols, radius_ref) for relative in range(2)]
    for start in range(0, half, STEP):
        rows = slice(start, start + STEP)
        anomalies = [mine_ref[i] for i in range(start, start + STEP)]
        for relative in range(2):
            totals[relative] = accumulate(
                totals[relative], plans[relative], anomalies, field_ref[0, rows, :], field_ref[1, rows, :], group * half + start
            )
    out_ref[0] = totals[0]
    out_ref[1] = totals[1]


def halo_kernel(tile_rows, place_ref, radius_ref, message_ref, own_ref, total_ref, send_ref):
    _, members, cols = message_ref.shape
    patch_cols = cols // PATCH
    group = place_ref[1]
    totals = [own_ref[0], own_ref[1]]
    plans = [taper_plan(group, relative, patch_cols, cols, radius_ref) for relative in range(2)]
    fields = []
    for k in range(2):
        rows = message_ref[FAR + k].astype(f32)
        fields.append(rows[:FAR] + rows[FAR : 2 * FAR])
    for start in range(0, FAR, STEP):
        anomalies = [message_ref[i] for i in range(start, start + STEP)]
        rows = slice(start, start + STEP)
        if start < NEAR:
            first = jnp.where(group == 0, -NEAR, tile_rows) + start
        else:
            first = jnp.where(group == 0, -FAR, tile_rows + NEAR) + start - NEAR
        for relative in range(2 if start < NEAR else 1):
            totals[relative] = accumulate(
                totals[relative], plans[relative], anomalies, fields[0][rows], fields[1][rows], first
            )
    sides = []
    pairs = patch_cols // 2
    for relative, total in enumerate(totals):
        patch_row = group if relative == 0 else 1 - group
        grams, side = [], []
        for pair in range(pairs):
            at = 2 * pair * members
            grams.append(jnp.concatenate([total[at : at + members], total[at + members : at + 2 * members]], 1))
            at = patch_cols * members + 2 * pair
            side.append(jnp.concatenate([total[at : at + 1], total[at + 1 : at + 2]], 1))
        sides.append(jnp.concatenate(side, 0))
        gram = jnp.concatenate(grams, 0)
        rows = pl.ds(pl.multiple_of(patch_row * (pairs * members), 16), pairs * members)
        total_ref[rows, :] = gram
        send_ref[rows, :] = gram.astype(bf16)
    side = jnp.concatenate(
        [jnp.where(group == 0, sides[0], sides[1]), jnp.where(group == 0, sides[1], sides[0])], 0
    )
    at = 2 * pairs * members
    total_ref[at:, :] = side
    send_ref[at:, :] = jnp.concatenate(split(side), 0)


def finish_kernel(total_ref, other_ref, lag_ref, mean_ref, out_ref, flat_ref):
    tile_rows, members, cols = lag_ref.shape
    degree = members - 1.0
    pair_count = total_ref.shape[0] // members
    grams_end = pair_count * members
    row = lax.broadcasted_iota(jnp.int32, (members, 2 * members), 0)
    lane = lax.broadcasted_iota(jnp.int32, (members, 2 * members), 1)
    identity = jnp.where(row == lane % members, 1.0, 0.0)
    left_mask = jnp.where(lane < members, 1.0, 0.0).astype(bf16)
    right_mask = jnp.where(lane < members, 0.0, 1.0).astype(bf16)

    def blocks(y):
        return jnp.concatenate([y * left_mask, y * right_mask], 0)

    def right(y):
        high, low = split(y)
        return blocks(high), blocks(low)

    def product(lefts, factor):
        high, low = factor
        rows = lefts[0][0].shape[0]
        first = mm(jnp.concatenate([part for pair in lefts for part in pair], 0), high)
        second = mm(jnp.concatenate([pair[0] for pair in lefts], 0), low)
        return [
            first[2 * k * rows : (2 * k + 1) * rows]
            + (first[(2 * k + 1) * rows : (2 * k + 2) * rows] + second[k * rows : (k + 1) * rows])
            for k in range(len(lefts))
        ]

    pairs = range(pair_count)
    grams = [
        total_ref[p * members : (p + 1) * members, :] + other_ref[p * members : (p + 1) * members, :].astype(f32)
        for p in pairs
    ]
    ends = [other_ref[grams_end + k * pair_count : grams_end + (k + 1) * pair_count, :].astype(f32) for k in range(2)]
    sides = total_ref[grams_end:, :] + (ends[0] + ends[1])
    squares = jnp.concatenate([jnp.sum(gram * gram, axis=0, keepdims=True) for gram in grams], 0)
    at_left = lax.broadcasted_iota(jnp.int32, squares.shape, 1) < members
    norm_left = jnp.sum(jnp.where(at_left, squares, 0.0), axis=1, keepdims=True)
    norm_right = jnp.sum(jnp.where(at_left, 0.0, squares), axis=1, keepdims=True)
    bound = degree + jnp.sqrt(jnp.where(at_left, norm_left, norm_right))
    spread = jnp.sqrt(degree / bound)
    iterates = [(grams[p] + degree * identity) / bound[p : p + 1] for p in pairs]
    corrections = [1.5 * identity - 0.5 * iterates[p] for p in pairs]
    factors = [right(corrections[p]) for p in pairs]
    iterates = [product([split(iterates[p])], factors[p])[0] for p in pairs]
    roots = corrections
    for step in range(1, NS_STEPS):
        halves = [split(roots[p]) for p in pairs]
        corrections = [1.5 * identity - 0.5 * product([halves[p]], right(iterates[p]))[0] for p in pairs]
        factors = [right(corrections[p]) for p in pairs]
        if step < NS_STEPS - 1:
            both = [product([split(iterates[p]), halves[p]], factors[p]) for p in pairs]
            iterates = [pair[0] for pair in both]
            roots = [pair[1] for pair in both]
        else:
            roots = [product([halves[p]], factors[p])[0] for p in pairs]
    mixings = []
    for p in pairs:
        factor = right(roots[p])
        side = jnp.broadcast_to(sides[p : p + 1], (PATCH, cols))
        inner = product([split(side)], factor)[0]
        weights = product([split(inner)], factor)[0][:1] / bound[p : p + 1]
        mixings.append((spread[p : p + 1] * roots[p] + weights).astype(bf16))

    patch = lax.broadcasted_iota(jnp.int32, (members, cols), 1) // PATCH
    even = jnp.where(patch % 2 == 0, 1.0, 0.0).astype(bf16)
    odd = jnp.where(patch % 2 == 1, 1.0, 0.0).astype(bf16)
    per_row = cols // (2 * PATCH)
    for a in range(tile_rows // PATCH):
        mixing = jnp.concatenate(mixings[a * per_row : (a + 1) * per_row], 0)
        for r in range(a * PATCH, (a + 1) * PATCH, 2):
            state = jnp.concatenate(
                [jnp.concatenate([lag_ref[i] * even, lag_ref[i] * odd], 0) for i in (r, r + 1)], 1
            )
            spread_out = mm(mixing, state)
            for i in (0, 1):
                part = spread_out[:, i * cols : (i + 1) * cols]
                chosen = part[:members]
                for pair in range(1, per_row):
                    chosen = jnp.where(patch // 2 == pair, part[pair * members : (pair + 1) * members], chosen)
                flat_ref[pl.ds(r + i, members, stride=tile_rows), :] = chosen + mean_ref[r + i : r + i + 1, :]
    out_ref[...] = flat_ref[...].reshape(1, members, tile_rows, cols).astype(bf16)


def shards(history, forecast, spot, alive, levels, precision, radius):
    shares = lax.axis_size("lag")
    tiles = lax.axis_size("dom")
    lag = lax.axis_index("lag")
    share_members, tile_rows, cols = forecast.shape
    members = share_members * shares
    patch_cols = cols // PATCH
    half = tile_rows // 2
    per_group = shares // 2
    place = jnp.stack([lag, lag // per_group])
    forward = [(t * shares, (t + 1) * shares) for t in range(tiles - 1)]
    halo_pairs = [(s + l, t + l) for s, t in forward for l in range(per_group)]
    halo_pairs += [(t + l, s + l) for s, t in forward for l in range(per_group, shares)]

    def call(kernel, name, in_specs, out_shape, scratch=()):
        return pl.pallas_call(
            kernel,
            in_specs=in_specs,
            out_specs=jax.tree.map(lambda _: vmem, out_shape),
            out_shape=out_shape,
            scratch_shapes=scratch,
            compiler_params=pltpu.CompilerParams(vmem_limit_bytes=32 * 2**20),
            name=name,
        )

    shape = jax.ShapeDtypeStruct
    smem = pl.BlockSpec(memory_space=pltpu.SMEM)
    vmem = pl.BlockSpec(memory_space=pltpu.VMEM)
    parts = [forecast]
    for k in range(1, shares):
        parts.append(lax.ppermute(forecast, "lag", [((i + k) % shares, i) for i in range(shares)]))
    fields, lag_rows, lag_mean = call(
        functools.partial(prepare_kernel, cols),
        "prepare",
        [smem, vmem, vmem, vmem, vmem],
        [
            shape((2, tile_rows, cols), f32),
            shape((tile_rows, members, cols), bf16),
            shape((tile_rows, cols), f32),
        ],
        [pltpu.VMEM((members * tile_rows, cols), f32)],
    )(alive, spot, levels, precision, history[0])
    mine, mine_field, message = call(
        functools.partial(pack_kernel, shares),
        "pack",
        [smem] + [vmem] * (shares + 1),
        [
            shape((half, members, cols), bf16),
            shape((2, half, cols), f32),
            shape((FAR + 2, members, cols), bf16),
        ],
        [pltpu.VMEM((members * tile_rows, cols), f32), pltpu.VMEM((2, tile_rows, cols), f32)],
    )(place, *parts, fields)
    message = lax.ppermute(message, ("dom", "lag"), halo_pairs)
    own = call(
        own_kernel,
        "own_gram",
        [smem, smem, vmem, vmem],
        shape((2, patch_cols * members + PATCH, members), f32),
    )(place, radius, mine, mine_field)
    pair_rows = patch_cols * members
    total, send = call(
        functools.partial(halo_kernel, tile_rows),
        "halo_gram",
        [smem, smem, vmem, vmem],
        [
            shape((pair_rows + patch_cols, 2 * members), f32),
            shape((pair_rows + 2 * patch_cols, 2 * members), bf16),
        ],
    )(place, radius, message, own)
    other = lax.ppermute(send, "lag", [(i, (i + per_group) % shares) for i in range(shares)])
    return call(
        finish_kernel,
        "finish",
        [vmem] * 4,
        shape((1, members, tile_rows, cols), bf16),
        [pltpu.VMEM((members * tile_rows, cols), f32)],
    )(total, other, lag_rows, lag_mean)


def solution(mesh):
    in_specs = (
        P("lag", None, "dom", None),
        P("lag", "dom", None),
        P("dom", None),
        P("dom"),
        P("dom", None),
        P("dom", None),
        P("dom"),
    )
    out_specs = P("lag", None, "dom", None)
    return jax.shard_map(shards, mesh=mesh, in_specs=in_specs, out_specs=out_specs, check_vma=False)
```

profile of v0, /device:TPU:8, one launch (start us, length us, event | category | flops | bytes accessed | tf_op | source)
XLA Modules:
  0.0 31.8 jit_solution(8605179668225299123)
XLA Ops:
  0.0 1.5 %collective-permute-start = (bf16[32,32,128]{2,1,0:T(8,128)(2,1)}, bf16[32,32,128]{2,1,0:T(8,128)(2,1)S(1)}, u32[]{:S(2)}, u32[]{:S(2)}) collective-permute-start(bf16[32,32,128]{2,1,0:T(8,128)(2,1)} %refs_0_.1), channel_id=1, source_target_pairs={{1,0},{0,1},{3,2},{2,3},{5,4},{4,5},{7,6},{6,7},{9,8},{8,9},{11,10... | collective-permute-start | bytes 786440 | tf_op jit(solution)/shard_map/ppermute | solution.py:316
  1.5 0.0 copy-start.6
  1.5 0.7 %copy-done.6 = s32[16]{0:T(128)S(1)} copy-done((s32[16]{0:T(128)S(1)}, s32[16]{0:T(128)}, u32[]{:S(2)}) %copy-start.6) | copy-done | bytes 88
  2.2 0.0 copy-start
  2.2 1.0 %copy-done = bf16[1,64,32,128]{3,2,1,0:T(8,128)(2,1)S(1)} copy-done((bf16[1,64,32,128]{3,2,1,0:T(8,128)(2,1)S(1)}, bf16[1,64,32,128]{3,2,1,0:T(8,128)(2,1)}, u32[]{:S(2)}) %copy-start) | copy-done | bytes 524312
  3.2 0.0 copy-start.2
  3.2 0.7 %copy-done.2 = s32[16,256]{1,0:T(8,128)S(1)} copy-done((s32[16,256]{1,0:T(8,128)S(1)}, s32[16,256]{1,0:T(8,128)}, u32[]{:S(2)}) %copy-start.2) | copy-done | bytes 16408
  3.9 0.0 copy-start.3
  3.9 0.7 %copy-done.3 = f32[16,256]{1,0:T(8,128)S(1)} copy-done((f32[16,256]{1,0:T(8,128)S(1)}, f32[16,256]{1,0:T(8,128)}, u32[]{:S(2)}) %copy-start.3) | copy-done | bytes 16408
  4.7 0.0 copy-start.4
  4.7 0.7 %copy-done.4 = f32[16,256]{1,0:T(8,128)S(1)} copy-done((f32[16,256]{1,0:T(8,128)S(1)}, f32[16,256]{1,0:T(8,128)}, u32[]{:S(2)}) %copy-start.4) | copy-done | bytes 16408
  5.4 0.0 copy-start.1
  5.4 1.6 %prepare.1 = (f32[2,32,128]{2,1,0:T(8,128)S(1)}, bf16[32,64,128]{2,1,0:T(8,128)(2,1)S(1)}, f32[32,128]{1,0:T(8,128)S(1)}) custom-call(s32[16]{0:T(128)S(1)} %copy-done.6, s32[16,256]{1,0:T(8,128)S(1)} %copy-done.2, f32[16,256]{1,0:T(8,128)S(1)} %copy-done.3, f32[16,256]{1,0:T(8,128)S(1)} %copy-done.4, bf16[64,32,128]{2,1,0:T(8,128)(2,1)S(1)} %bitcast.2), custom_call_target="tpu_custom_call" | custom-call | tf_op jit(solution)/shard_map/prepare/pallas_call | solution.py:317
  7.0 0.1 pad_add_fusion.place_ref
  7.1 1.2 %collective-permute-done.refs_1_ = bf16[32,32,128]{2,1,0:T(8,128)(2,1)S(1)} collective-permute-done((bf16[32,32,128]{2,1,0:T(8,128)(2,1)}, bf16[32,32,128]{2,1,0:T(8,128)(2,1)S(1)}, u32[]{:S(2)}, u32[]{:S(2)}) %collective-permute-start) | collective-permute-done | bytes 262176 | tf_op jit(solution)/shard_map/ppermute | solution.py:316
  8.3 0.0 copy-done.1
  8.3 1.4 %pack.1 = (bf16[16,64,128]{2,1,0:T(8,128)(2,1)S(1)}, f32[2,16,128]{2,1,0:T(8,128)S(1)}, bf16[26,64,128]{2,1,0:T(8,128)(2,1)S(1)}) custom-call(s32[2]{0:T(128)S(1)} %pad_add_fusion.place_ref, bf16[32,32,128]{2,1,0:T(8,128)(2,1)S(1)} %copy-done.1, bf16[32,32,128]{2,1,0:T(8,128)(2,1)S(1)} %collective-permute-done.refs_1_, ...), custom_call_target="tpu_custom_call" | custom-call | tf_op jit(solution)/shard_map/pack/pallas_call | solution.py:328
  9.7 1.9 %collective-permute-start.1 = (bf16[26,64,128]{2,1,0:T(8,128)(2,1)S(1)}, bf16[26,64,128]{2,1,0:T(8,128)(2,1)S(1)}, u32[]{:S(2)}, u32[]{:S(2)}) collective-permute-start(bf16[26,64,128]{2,1,0:T(8,128)(2,1)S(1)} %get-tuple-element.14), channel_id=1, source_target_pairs={{0,2},{2,4},{4,6},{6,8},{8,10},{10,12},{12,14},{14,16},{16,18},{18... | collective-permute-start | bytes 1277960 | tf_op jit(solution)/shard_map/ppermute | solution.py:339
  11.6 0.0 copy-start.5
  11.7 0.6 %copy-done.5 = s32[16]{0:T(128)S(1)} copy-done((s32[16]{0:T(128)S(1)}, s32[16]{0:T(128)}, u32[]{:S(2)}) %copy-start.5) | copy-done | bytes 88
  12.3 1.8 %own_gram.1.own_ref = f32[2,528,64]{2,1,0:T(8,128)S(1)} custom-call(s32[2]{0:T(128)S(1)} %pad_add_fusion.place_ref, s32[16]{0:T(128)S(1)} %copy-done.5, bf16[16,64,128]{2,1,0:T(8,128)(2,1)S(1)} %get-tuple-element.15.mine_ref, f32[2,16,128]{2,1,0:T(8,128)S(1)} %get-tuple-element.16.field_ref), custom_call_target="tpu_custom_call" | custom-call | tf_op jit(solution)/shard_map/own_gram/pallas_call | solution.py:340
  14.1 5.9 %collective-permute-done.1.message_ref = bf16[26,64,128]{2,1,0:T(8,128)(2,1)S(1)} collective-permute-done((bf16[26,64,128]{2,1,0:T(8,128)(2,1)S(1)}, bf16[26,64,128]{2,1,0:T(8,128)(2,1)S(1)}, u32[]{:S(2)}, u32[]{:S(2)}) %collective-permute-start.1) | collective-permute-done | bytes 426016 | tf_op jit(solution)/shard_map/ppermute | solution.py:339
  20.1 1.9 %halo_gram.1 = (f32[520,128]{1,0:T(8,128)S(1)}, bf16[528,128]{1,0:T(8,128)(2,1)S(1)}) custom-call(s32[2]{0:T(128)S(1)} %pad_add_fusion.place_ref, s32[16]{0:T(128)S(1)} %copy-done.5, bf16[26,64,128]{2,1,0:T(8,128)(2,1)S(1)} %collective-permute-done.1.message_ref, f32[2,528,64]{2,1,0:T(8,128)S(1)} %own_gram.1.own_ref), custom_call_target="tpu_custom_call" | custom-call | tf_op jit(solution)/shard_map/halo_gram/pallas_call | solution.py:347
  22.0 0.1 collective-permute-start.2
  22.1 5.0 %collective-permute-done.2.other_ref = bf16[528,128]{1,0:T(8,128)(2,1)S(1)} collective-permute-done((bf16[528,128]{1,0:T(8,128)(2,1)S(1)}, bf16[528,128]{1,0:T(8,128)(2,1)S(1)}, u32[]{:S(2)}, u32[]{:S(2)}) %collective-permute-start.2) | collective-permute-done | bytes 135200 | tf_op jit(solution)/shard_map/ppermute | solution.py:356
  27.1 4.7 %finish.1 = bf16[1,64,32,128]{3,2,1,0:T(8,128)(2,1)} custom-call(f32[520,128]{1,0:T(8,128)S(1)} %get-tuple-element.17.total_ref, bf16[528,128]{1,0:T(8,128)(2,1)S(1)} %collective-permute-done.2.other_ref, bf16[32,64,128]{2,1,0:T(8,128)(2,1)S(1)} %get-tuple-element.19.lag_ref, f32[32,128]{1,0:T(8,128)S(1)} %get-tuple-element.20.mean_ref), custom_call_target="tpu_custom_call" | custom-call | tf_op jit(solution)/shard_map/finish/pallas_call | solution.py:357
Async XLA Ops:
  0.0 8.3 %collective-permute-start = (bf16[32,32,128]{2,1,0:T(8,128)(2,1)}, bf16[32,32,128]{2,1,0:T(8,128)(2,1)S(1)}, u32[]{:S(2)}, u32[]{:S(2)}) collective-permute-start(bf16[32,32,128]{2,1,0:T(8,128)(2,1)} %refs_0_.1), channel_id=1, source_target_pairs={{1,0},{0,1},{3,2},{2,3},{5,4},{4,5},{7,6},{6,7},{9,8},{8,9},{11,10... | collective-permute-start | bytes 786440 | tf_op jit(solution)/shard_map/ppermute | solution.py:316
  1.5 0.7 %copy-start.6 = (s32[16]{0:T(128)S(1)}, s32[16]{0:T(128)}, u32[]{:S(2)}) copy-start(s32[16]{0:T(128)} %alive_ref.1) | copy-start | bytes 196
  2.2 1.0 %copy-start = (bf16[1,64,32,128]{3,2,1,0:T(8,128)(2,1)S(1)}, bf16[1,64,32,128]{3,2,1,0:T(8,128)(2,1)}, u32[]{:S(2)}) copy-start(bf16[1,64,32,128]{3,2,1,0:T(8,128)(2,1)} %param.7) | copy-start | bytes 1572868
  3.2 0.7 %copy-start.2 = (s32[16,256]{1,0:T(8,128)S(1)}, s32[16,256]{1,0:T(8,128)}, u32[]{:S(2)}) copy-start(s32[16,256]{1,0:T(8,128)} %spot_ref.1) | copy-start | bytes 49156
  3.9 0.7 %copy-start.3 = (f32[16,256]{1,0:T(8,128)S(1)}, f32[16,256]{1,0:T(8,128)}, u32[]{:S(2)}) copy-start(f32[16,256]{1,0:T(8,128)} %level_ref.1) | copy-start | bytes 49156
  4.7 0.7 %copy-start.4 = (f32[16,256]{1,0:T(8,128)S(1)}, f32[16,256]{1,0:T(8,128)}, u32[]{:S(2)}) copy-start(f32[16,256]{1,0:T(8,128)} %prec_ref.1) | copy-start | bytes 49156
  5.4 2.9 %copy-start.1 = (bf16[32,32,128]{2,1,0:T(8,128)(2,1)S(1)}, bf16[32,32,128]{2,1,0:T(8,128)(2,1)}, u32[]{:S(2)}) copy-start(bf16[32,32,128]{2,1,0:T(8,128)(2,1)} %refs_0_.1) | copy-start | bytes 786436
  9.7 10.3 %collective-permute-start.1 = (bf16[26,64,128]{2,1,0:T(8,128)(2,1)S(1)}, bf16[26,64,128]{2,1,0:T(8,128)(2,1)S(1)}, u32[]{:S(2)}, u32[]{:S(2)}) collective-permute-start(bf16[26,64,128]{2,1,0:T(8,128)(2,1)S(1)} %get-tuple-element.14), channel_id=1, source_target_pairs={{0,2},{2,4},{4,6},{6,8},{8,10},{10,12},{12,14},{14,16},{16,18},{18... | collective-permute-start | bytes 1277960 | tf_op jit(solution)/shard_map/ppermute | solution.py:339
  11.6 0.7 %copy-start.5 = (s32[16]{0:T(128)S(1)}, s32[16]{0:T(128)}, u32[]{:S(2)}) copy-start(s32[16]{0:T(128)} %radius_ref.3) | copy-start | bytes 196
  22.0 5.1 %collective-permute-start.2 = (bf16[528,128]{1,0:T(8,128)(2,1)S(1)}, bf16[528,128]{1,0:T(8,128)(2,1)S(1)}, u32[]{:S(2)}, u32[]{:S(2)}) collective-permute-start(bf16[528,128]{1,0:T(8,128)(2,1)S(1)} %get-tuple-element.18), channel_id=1, source_target_pairs={{0,1},{1,0},{2,3},{3,2},{4,5},{5,4},{6,7},{7,6},{8,9},{9,8},{10,11... | collective-permute-start | bytes 405512 | tf_op jit(solution)/shard_map/ppermute | solution.py:356
where the time goes:
time: 32.2 us; the launch traced here: 31.8 us
  waiting for transfers between devices  12.1 us (38%)
  Pallas kernels  11.5 us (36%)
  local copies, waits for them, and re-layouts  4.5 us (14%)
  starting transfers between devices  3.51 us (11%)
    ppermute x1, waiting for transfers between devices, shards(): message = lax.ppermute(message, ('dom', 'lag'), halo_pairs)  5.93 us
    ppermute x1, waiting for transfers between devices, shards(): lax.ppermute(send, 'lag', [(i, (i + per_group) % shares) for i in range(s...  5 us
    pallas_call x1, Pallas kernels, shards(): call(finish_kernel, 'finish', [vmem] * 4, shape((1, members, tile_rows, c...  4.71 us
    unnamed x14, local copies, waits for them, and re-layouts  4.5 us
    ppermute x1, starting transfers between devices, shards(): message = lax.ppermute(message, ('dom', 'lag'), halo_pairs)  1.92 us
    pallas_call x1, Pallas kernels, shards(): call(functools.partial(halo_kernel, tile_rows), 'halo_gram', [smem, smem,...  1.91 us
    pallas_call x1, Pallas kernels, shards(): call(own_kernel, 'own_gram', [smem, smem, vmem, vmem], shape((2, patch_co...  1.82 us
    pallas_call x1, Pallas kernels, shards(): call(functools.partial(prepare_kernel, cols), 'prepare', [smem, vmem, vme...  1.62 us
  transfers between devices with their start and end apart: 3, of which 3 were waited for; matrix products, arithmetic and copies ran while one was open for 0% of the time, Pallas kernels for 11%

commit v1 on v0

--- a/solution.py
+++ b/solution.py
@@ -12,6 +12,7 @@
 RADIUS = 32
 FAR = RADIUS - PATCH // 2
 NEAR = FAR - PATCH
+MIDDLE = (PATCH - 1) / 2
 
 NT = (((1,), (1,)), ((), ()))
 NN = (((1,), (0,)), ((), ()))
@@ -28,7 +29,17 @@
     return high, (x - high.astype(f32)).astype(bf16)
 
 
-def prepare_kernel(cols, alive_ref, spot_ref, level_ref, prec_ref, hist_ref, field_ref, lag_ref, mean_ref, flat_ref):
+def fields_kernel(cols, alive_hbm, spot_hbm, level_hbm, prec_hbm, field_ref, alive_ref, spot_ref, level_ref, prec_ref, sem):
+    copies = [
+        pltpu.make_async_copy(source, target, sem.at[k])
+        for k, (source, target) in enumerate(
+            ((alive_hbm, alive_ref), (spot_hbm, spot_ref), (level_hbm, level_ref), (prec_hbm, prec_ref))
+        )
+    ]
+    for copy in copies:
+        copy.start()
+    for copy in copies:
+        copy.wait()
     patches, slots = spot_ref.shape
     patch_cols = cols // PATCH
     patch_rows = patches // patch_cols
@@ -56,7 +67,13 @@
         rows = slice(a * PATCH, (a + 1) * PATCH)
         field_ref[0, rows, :] = total[:PATCH] + total[PATCH : 2 * PATCH]
         field_ref[1, rows, :] = total[2 * PATCH : 3 * PATCH] + total[3 * PATCH :]
-    members, tile_rows, _ = hist_ref.shape
+
+
+def state_kernel(after_ref, hist_hbm, lag_ref, mean_ref, hist_ref, flat_ref, sem):
+    copy = pltpu.make_async_copy(hist_hbm, hist_ref, sem)
+    copy.start()
+    copy.wait()
+    members, tile_rows, cols = hist_ref.shape
     state = hist_ref[...].astype(f32)
     mean = jnp.sum(state, axis=0) / members
     mean_ref[...] = mean
@@ -65,53 +82,14 @@
         lag_ref[r] = flat_ref[pl.ds(r, members, stride=tile_rows), :].astype(bf16)
 
 
-def pack_kernel(shares, place_ref, *refs):
-    parts, refs = refs[:shares], refs[shares:]
-    field_ref, mine_ref, mine_field_ref, message_ref, flat_ref, held_ref = refs
-    share_members, tile_rows, cols = parts[0].shape
-    members = share_members * shares
-    lag, group = place_ref[0], place_ref[1]
-    states = [part[...].astype(f32) for part in parts]
-    mean = functools.reduce(jnp.add, [jnp.sum(state, axis=0) for state in states]) / members
-    for k, state in enumerate(states):
-        at = pl.multiple_of(lax.rem(lag + k, shares) * (share_members * tile_rows), 8)
-        flat_ref[pl.ds(at, share_members * tile_rows), :] = (state - mean[None]).reshape(-1, cols)
-    weight = field_ref[0]
-    held_ref[0] = weight
-    held_ref[1] = field_ref[1] - mean * weight
-
-    def row(r):
-        return flat_ref[pl.ds(r, members, stride=tile_rows), :].astype(bf16)
-
-    half = mine_ref.shape[0]
-    first = pl.multiple_of(group * half, 8)
-    for i in range(half):
-        mine_ref[i] = row(first + i)
-    mine_field_ref[0] = held_ref[0, pl.ds(first, half), :]
-    mine_field_ref[1] = held_ref[1, pl.ds(first, half), :]
-    near = pl.multiple_of((1 - group) * (tile_rows - NEAR), 8)
-    far = tile_rows - FAR
-    for i in range(NEAR):
-        message_ref[i] = row(near + i)
-    for i in range(FAR - NEAR):
-        message_ref[NEAR + i] = row(far + i)
-    for k in range(2):
-        rows = jnp.concatenate([held_ref[k, pl.ds(near, NEAR), :], held_ref[k, far : far + FAR - NEAR, :]], 0)
-        high, low = split(rows)
-        rest = jnp.zeros((members - 2 * FAR, cols), bf16)
-        message_ref[FAR + k] = jnp.concatenate([high, low, rest], 0)
-
-
-def taper_plan(group, relative, patch_cols, cols, radius_ref):
-    patch_row = group if relative == 0 else 1 - group
+def taper_plan(centre_row, first_patch, patch_cols, cols, radius_ref):
     q_row = lax.broadcasted_iota(jnp.int32, (patch_cols, cols), 0)
     col = lax.broadcasted_iota(jnp.int32, (patch_cols, cols), 1)
     radius = jnp.zeros((patch_cols, cols), f32)
     for q in range(patch_cols):
-        radius = jnp.where(q_row == q, radius_ref[patch_row * patch_cols + q].astype(f32), radius)
-    middle = (PATCH - 1) / 2
-    col_square = jnp.square(col.astype(f32) - (q_row.astype(f32) * PATCH + middle))
-    return patch_row.astype(f32) * PATCH + middle, col_square, 1.0 / jnp.square(radius)
+        radius = jnp.where(q_row == q, radius_ref[first_patch + q].astype(f32), radius)
+    col_square = jnp.square(col.astype(f32) - (q_row.astype(f32) * PATCH + MIDDLE))
+    return centre_row, col_square, 1.0 / jnp.square(radius)
 
 
 def accumulate(total, plan, anomalies, weight, innovation, first_row):
@@ -137,65 +115,98 @@
 STEP = 8
 
 
-def own_kernel(place_ref, radius_ref, mine_ref, field_ref, out_ref):
-    half, members, cols = mine_ref.shape
-    patch_cols = cols // PATCH
-    group = place_ref[1]
-    totals = [jnp.zeros(out_ref.shape[1:], f32) for _ in range(2)]
-    plans = [taper_plan(group, relative, patch_cols, cols, radius_ref) for relative in range(2)]
-    for start in range(0, half, STEP):
-        rows = slice(start, start + STEP)
-        anomalies = [mine_ref[i] for i in range(start, start + STEP)]
-        for relative in range(2):
-            totals[relative] = accumulate(
-                totals[relative], plans[relative], anomalies, field_ref[0, rows, :], field_ref[1, rows, :], group * half + start
-            )
-    out_ref[0] = totals[0]
-    out_ref[1] = totals[1]
-
-
-def halo_kernel(tile_rows, place_ref, radius_ref, message_ref, own_ref, total_ref, send_ref):
-    _, members, cols = message_ref.shape
-    patch_cols = cols // PATCH
-    group = place_ref[1]
-    totals = [own_ref[0], own_ref[1]]
-    plans = [taper_plan(group, relative, patch_cols, cols, radius_ref) for relative in range(2)]
-    fields = []
-    for k in range(2):
-        rows = message_ref[FAR + k].astype(f32)
-        fields.append(rows[:FAR] + rows[FAR : 2 * FAR])
-    for start in range(0, FAR, STEP):
-        anomalies = [message_ref[i] for i in range(start, start + STEP)]
-        rows = slice(start, start + STEP)
-        if start < NEAR:
-            first = jnp.where(group == 0, -NEAR, tile_rows) + start
-        else:
-            first = jnp.where(group == 0, -FAR, tile_rows + NEAR) + start - NEAR
-        for relative in range(2 if start < NEAR else 1):
-            totals[relative] = accumulate(
-                totals[relative], plans[relative], anomalies, fields[0][rows], fields[1][rows], first
-            )
-    sides = []
+def paired(totals, members, patch_cols):
     pairs = patch_cols // 2
-    for relative, total in enumerate(totals):
-        patch_row = group if relative == 0 else 1 - group
-        grams, side = [], []
+    grams, sides = [], []
+    for total in totals:
         for pair in range(pairs):
             at = 2 * pair * members
             grams.append(jnp.concatenate([total[at : at + members], total[at + members : at + 2 * members]], 1))
+        for pair in range(pairs):
             at = patch_cols * members + 2 * pair
-            side.append(jnp.concatenate([total[at : at + 1], total[at + 1 : at + 2]], 1))
-        sides.append(jnp.concatenate(side, 0))
-        gram = jnp.concatenate(grams, 0)
-        rows = pl.ds(pl.multiple_of(patch_row * (pairs * members), 16), pairs * members)
-        total_ref[rows, :] = gram
-        send_ref[rows, :] = gram.astype(bf16)
-    side = jnp.concatenate(
-        [jnp.where(group == 0, sides[0], sides[1]), jnp.where(group == 0, sides[1], sides[0])], 0
-    )
-    at = 2 * pairs * members
-    total_ref[at:, :] = side
-    send_ref[at:, :] = jnp.concatenate(split(side), 0)
+            sides.append(jnp.concatenate([total[at : at + 1], total[at + 1 : at + 2]], 1))
+    return jnp.concatenate(grams, 0), jnp.concatenate(sides, 0)
+
+
+def message_of(grams, sides):
+    return jnp.concatenate([grams.astype(bf16), *split(sides)], 0)
+
+
+def read_message(ref, side_count):
+    at = ref.shape[0] - 2 * side_count
+    high, low = ref[at : at + side_count, :].astype(f32), ref[at + side_count :, :].astype(f32)
+    return jnp.concatenate([ref[:at, :].astype(f32), high + low], 0)
+
+
+def outward_kernel(shares, place_ref, radius_ref, *refs):
+    parts, refs = refs[:shares], refs[shares:]
+    field_ref, near_ref, far_ref, held_ref, message_ref, flat_ref, total_ref = refs
+    share_members, tile_rows, cols = parts[0].shape
+    members = share_members * shares
+    patch_cols = cols // PATCH
+    lag, group = place_ref[0], place_ref[1]
+    states = [part[...].astype(f32) for part in parts]
+    mean = functools.reduce(jnp.add, [jnp.sum(state, axis=0) for state in states]) / members
+    for k, state in enumerate(states):
+        at = pl.multiple_of(lax.rem(lag + k, shares) * (share_members * tile_rows), 8)
+        flat_ref[pl.ds(at, share_members * tile_rows), :] = (state - mean[None]).reshape(-1, cols)
+    weight = field_ref[0]
+    held_ref[0] = weight
+    held_ref[1] = field_ref[1] - mean * weight
+
+    def row(r):
+        return flat_ref[pl.ds(r, members, stride=tile_rows), :].astype(bf16)
+
+    near = pl.multiple_of(group * (tile_rows - NEAR), 8)
+    sign = 1 - 2 * group
+    middle = jnp.where(group == 0, MIDDLE - PATCH, MIDDLE + tile_rows)
+    first_near = (1 - group) * patch_cols
+    plans = [
+        taper_plan(middle, first_near, patch_cols, cols, radius_ref),
+        taper_plan(middle - (sign * PATCH).astype(f32), patch_cols - first_near, patch_cols, cols, radius_ref),
+    ]
+    anomalies = [row(near + i) for i in range(NEAR)]
+    for i, anomaly in enumerate(anomalies):
+        near_ref[i] = anomaly
+    weights, innovations = (held_ref[k, pl.ds(near, NEAR), :] for k in range(2))
+    blank = jnp.zeros(total_ref.shape[1:], f32)
+    totals = [accumulate(blank, plan, anomalies, weights, innovations, near) for plan in plans]
+    for start in range(NEAR, FAR, STEP):
+        anomalies = [row(start + i) for i in range(STEP)]
+        for i, anomaly in enumerate(anomalies):
+            far_ref[start - NEAR + i] = anomaly
+        rows = slice(start, start + STEP)
+        totals[0] = accumulate(totals[0], plans[0], anomalies, held_ref[0, rows, :], held_ref[1, rows, :], jnp.int32(start))
+    total_ref[1 - group] = totals[0]
+    total_ref[group] = totals[1]
+    message_ref[...] = message_of(*paired([total_ref[0], total_ref[1]], members, patch_cols))
+
+
+def own_kernel(place_ref, radius_ref, near_ref, far_ref, field_ref, out_ref):
+    members, cols = near_ref.shape[1:]
+    tile_rows = field_ref.shape[1]
+    patch_cols = cols // PATCH
+    group = place_ref[1]
+    plans = [
+        taper_plan(MIDDLE + a * PATCH, a * patch_cols, patch_cols, cols, radius_ref) for a in range(tile_rows // PATCH)
+    ]
+    near = pl.multiple_of(group * (tile_rows - NEAR), 8)
+    far = pl.multiple_of(NEAR + group * (FAR - 2 * NEAR), 8)
+    totals = [jnp.zeros((patch_cols * members + PATCH, members), f32) for _ in plans]
+    for first, anomalies in (
+        (near, [near_ref[i] for i in range(NEAR)]),
+        (far, [far_ref[far - NEAR + i] for i in range(tile_rows // 2 - NEAR)]),
+    ):
+        fields = [field_ref[k, pl.ds(first, len(anomalies)), :] for k in range(2)]
+        totals = [accumulate(total, plan, anomalies, *fields, first) for total, plan in zip(totals, plans)]
+    out_ref[...] = jnp.concatenate(paired(totals, members, patch_cols), 0)
+
+
+def join_kernel(own_ref, message_ref, total_ref, send_ref):
+    sides = message_ref.shape[0] - own_ref.shape[0]
+    total = own_ref[...] + read_message(message_ref, sides)
+    total_ref[...] = total
+    send_ref[...] = message_of(total[: total.shape[0] - sides], total[total.shape[0] - sides :])
 
 
 def finish_kernel(total_ref, other_ref, lag_ref, mean_ref, out_ref, flat_ref):
@@ -228,12 +239,9 @@
         ]
 
     pairs = range(pair_count)
-    grams = [
-        total_ref[p * members : (p + 1) * members, :] + other_ref[p * members : (p + 1) * members, :].astype(f32)
-        for p in pairs
-    ]
-    ends = [other_ref[grams_end + k * pair_count : grams_end + (k + 1) * pair_count, :].astype(f32) for k in range(2)]
-    sides = total_ref[grams_end:, :] + (ends[0] + ends[1])
+    total = total_ref[...] + read_message(other_ref, pair_count)
+    grams = [total[p * members : (p + 1) * members] for p in pairs]
+    sides = total[grams_end:]
     squares = jnp.concatenate([jnp.sum(gram * gram, axis=0, keepdims=True) for gram in grams], 0)
     at_left = lax.broadcasted_iota(jnp.int32, squares.shape, 1) < members
     norm_left = jnp.sum(jnp.where(at_left, squares, 0.0), axis=1, keepdims=True)
@@ -290,12 +298,11 @@
     share_members, tile_rows, cols = forecast.shape
     members = share_members * shares
     patch_cols = cols // PATCH
-    half = tile_rows // 2
     per_group = shares // 2
     place = jnp.stack([lag, lag // per_group])
     forward = [(t * shares, (t + 1) * shares) for t in range(tiles - 1)]
-    halo_pairs = [(s + l, t + l) for s, t in forward for l in range(per_group)]
-    halo_pairs += [(t + l, s + l) for s, t in forward for l in range(per_group, shares)]
+    halo_pairs = [(t + l, s + l) for s, t in forward for l in range(per_group)]
+    halo_pairs += [(s + l, t + l) for s, t in forward for l in range(per_group, shares)]
 
     def call(kernel, name, in_specs, out_shape, scratch=()):
         return pl.pallas_call(
@@ -311,48 +318,67 @@
     shape = jax.ShapeDtypeStruct
     smem = pl.BlockSpec(memory_space=pltpu.SMEM)
     vmem = pl.BlockSpec(memory_space=pltpu.VMEM)
+    hbm = pl.BlockSpec(memory_space=pltpu.HBM)
     parts = [forecast]
     for k in range(1, shares):
         parts.append(lax.ppermute(forecast, "lag", [((i + k) % shares, i) for i in range(shares)]))
-    fields, lag_rows, lag_mean = call(
-        functools.partial(prepare_kernel, cols),
-        "prepare",
-        [smem, vmem, vmem, vmem, vmem],
+    next_radius = lax.ppermute(radius, ("dom", "lag"), [(s, t) for t, s in halo_pairs])
+    fields = call(
+        functools.partial(fields_kernel, cols),
+        "fields",
+        [hbm] * 4,
+        shape((2, tile_rows, cols), f32),
         [
+            pltpu.SMEM(alive.shape, jnp.int32),
+            pltpu.VMEM(spot.shape, jnp.int32),
+            pltpu.VMEM(levels.shape, f32),
+            pltpu.VMEM(precision.shape, f32),
+            pltpu.SemaphoreType.DMA((4,)),
+        ],
+    )(alive, spot, levels, precision)
+    pair_rows = patch_cols * members
+    near, far, held, message = call(
+        functools.partial(outward_kernel, shares),
+        "outward_gram",
+        [smem, smem] + [vmem] * (shares + 1),
+        [
+            shape((NEAR, members, cols), bf16),
+            shape((FAR - NEAR, members, cols), bf16),
             shape((2, tile_rows, cols), f32),
-            shape((tile_rows, members, cols), bf16),
-            shape((tile_rows, cols), f32),
+            shape((pair_rows + 2 * patch_cols, 2 * members), bf16),
         ],
-        [pltpu.VMEM((members * tile_rows, cols), f32)],
-    )(alive, spot, levels, precision, history[0])
-    mine, mine_field, message = call(
-        functools.partial(pack_kernel, shares),
-        "pack",
-        [smem] + [vmem] * (shares + 1),
         [
-            shape((half, members, cols), bf16),
-            shape((2, half, cols), f32),
-            shape((FAR + 2, members, cols), bf16),
+            pltpu.VMEM((members * tile_rows, cols), f32),
+            pltpu.VMEM((2, patch_cols * members + PATCH, members), f32),
         ],
-        [pltpu.VMEM((members * tile_rows, cols), f32), pltpu.VMEM((2, tile_rows, cols), f32)],
-    )(place, *parts, fields)
+    )(place, next_radius, *parts, fields)
     message = lax.ppermute(message, ("dom", "lag"), halo_pairs)
     own = call(
         own_kernel,
         "own_gram",
-        [smem, smem, vmem, vmem],
-        shape((2, patch_cols * members + PATCH, members), f32),
-    )(place, radius, mine, mine_field)
-    pair_rows = patch_cols * members
+        [smem, smem] + [vmem] * 3,
+        shape((pair_rows + patch_cols, 2 * members), f32),
+    )(place, radius, near, far, held)
+    lag_rows, lag_mean = call(
+        state_kernel,
+        "state",
+        [hbm, hbm],
+        [shape((tile_rows, members, cols), bf16), shape((tile_rows, cols), f32)],
+        [
+            pltpu.VMEM((members, tile_rows, cols), bf16),
+            pltpu.VMEM((members * tile_rows, cols), f32),
+            pltpu.SemaphoreType.DMA,
+        ],
+    )(held, history[0])
     total, send = call(
-        functools.partial(halo_kernel, tile_rows),
-        "halo_gram",
-        [smem, smem, vmem, vmem],
+        join_kernel,
+        "join",
+        [vmem, vmem],
         [
             shape((pair_rows + patch_cols, 2 * members), f32),
             shape((pair_rows + 2 * patch_cols, 2 * members), bf16),
         ],
-    )(place, radius, message, own)
+    )(own, message)
     other = lax.ppermute(send, "lag", [(i, (i + per_group) % shares) for i in range(shares)])
     return call(
         finish_kernel,

time: 32.2 us -> 29.1 us (0.904)
  waiting for transfers between devices: 12.1 us -> 3.91 us
  starting transfers between devices: 3.51 us -> 9.67 us
  Pallas kernels: 11.5 us -> 10.6 us
    ppermute x1, waiting for transfers between devices: 5.93 us -> 0.01 us  [shards(): message = lax.ppermute(message, ('dom', 'lag'), halo_pairs)]
    ppermute x1, starting transfers between devices: 0.07 us -> 2.63 us  [shards(): lax.ppermute(send, 'lag', [(i, (i + per_group) % shares) for i in range(s...]
    ppermute x1, waiting for transfers between devices: 5 us -> 2.95 us  [shards(): lax.ppermute(send, 'lag', [(i, (i + per_group) % shares) for i in range(s...]
    ppermute x0 -> x1, starting transfers between devices: none -> 1.91 us  [shards(): lax.ppermute(radius, ('dom', 'lag'), [(s, t) for t, s in halo_pairs])]
    ppermute x1, starting transfers between devices: 1.92 us -> 3.61 us  [shards(): message = lax.ppermute(message, ('dom', 'lag'), halo_pairs)]
    pallas_call x4 -> x5, Pallas kernels: 6.79 us -> 5.88 us  [the longest x1 2.13 us: shards(): call(functools.partial(outward_kernel, shares), 'outward_gram', [smem, sm...]
    ppermute x1, waiting for transfers between devices: 1.18 us -> 0.85 us  [shards(): lax.ppermute(forecast, 'lag', [((i + k) % shares, i) for i in range(share...]
  transfers between devices with their start and end apart: 3 -> 4, of which waited for: 3 -> 3; matrix products, arithmetic and copies ran while one was open for 0% -> 0% of each run, Pallas kernels for 11% -> 13%
where the time goes in v1:
time: 29.1 us; the launch traced here: 28.7 us
  Pallas kernels  10.6 us (36%)
  starting transfers between devices  9.67 us (33%)
  local copies, waits for them, and re-layouts  4.33 us (15%)
  waiting for transfers between devices  3.91 us (13%)
    pallas_call x1, Pallas kernels, shards(): call(finish_kernel, 'finish', [vmem] * 4, shape((1, members, tile_rows, c...  4.7 us
    unnamed x14, local copies, waits for them, and re-layouts  4.33 us
    ppermute x1, starting transfers between devices, shards(): message = lax.ppermute(message, ('dom', 'lag'), halo_pairs)  3.61 us
    ppermute x1, waiting for transfers between devices, shards(): lax.ppermute(send, 'lag', [(i, (i + per_group) % shares) for i in range(s...  2.95 us
    ppermute x1, starting transfers between devices, shards(): lax.ppermute(send, 'lag', [(i, (i + per_group) % shares) for i in range(s...  2.63 us
    pallas_call x1, Pallas kernels, shards(): call(functools.partial(outward_kernel, shares), 'outward_gram', [smem, sm...  2.13 us
    ppermute x1, starting transfers between devices, shards(): lax.ppermute(radius, ('dom', 'lag'), [(s, t) for t, s in halo_pairs])  1.91 us
    pallas_call x1, Pallas kernels, shards(): call(own_kernel, 'own_gram', [smem, smem] + [vmem] * 3, shape((pair_rows...  1.89 us
  transfers between devices with their start and end apart: 4, of which 3 were waited for; matrix products, arithmetic and copies ran while one was open for 0% of the time, Pallas kernels for 13%

profile of v1, /device:TPU:8, one launch (start us, length us, event | category | flops | bytes accessed | tf_op | source)
XLA Modules:
  0.0 28.7 jit_solution(12920661801022920257)
XLA Ops:
  0.0 1.5 %collective-permute-start.1 = (bf16[32,32,128]{2,1,0:T(8,128)(2,1)}, bf16[32,32,128]{2,1,0:T(8,128)(2,1)S(1)}, u32[]{:S(2)}, u32[]{:S(2)}) collective-permute-start(bf16[32,32,128]{2,1,0:T(8,128)(2,1)} %refs_0_.1), channel_id=1, source_target_pairs={{1,0},{0,1},{3,2},{2,3},{5,4},{4,5},{7,6},{6,7},{9,8},{8,9},{11,10... | collective-permute-start | bytes 786440 | tf_op jit(solution)/shard_map/ppermute | solution.py:324
  1.5 1.9 %collective-permute-start = (s32[16]{0:T(128)}, s32[16]{0:T(128)S(1)}, u32[]{:S(2)}, u32[]{:S(2)}) collective-permute-start(s32[16]{0:T(128)} %radius_ref.1), channel_id=1, source_target_pairs={{0,2},{2,4},{4,6},{6,8},{8,10},{10,12},{12,14},{14,16},{16,18},{18... | collective-permute-start | bytes 200 | tf_op jit(solution)/shard_map/ppermute | solution.py:325
  3.4 0.0 copy-start.5
  3.5 0.1 pad_add_fusion.place_ref
  3.5 0.6 %copy-done.5 = s32[16]{0:T(128)S(1)} copy-done((s32[16]{0:T(128)S(1)}, s32[16]{0:T(128)}, u32[]{:S(2)}) %copy-start.5) | copy-done | bytes 88
  4.1 0.0 copy-start.2
  4.1 0.7 %copy-done.2 = s32[16,256]{1,0:T(8,128)S(1)} copy-done((s32[16,256]{1,0:T(8,128)S(1)}, s32[16,256]{1,0:T(8,128)}, u32[]{:S(2)}) %copy-start.2) | copy-done | bytes 16408
  4.8 0.0 copy-start.3
  4.8 0.7 %copy-done.3 = f32[16,256]{1,0:T(8,128)S(1)} copy-done((f32[16,256]{1,0:T(8,128)S(1)}, f32[16,256]{1,0:T(8,128)}, u32[]{:S(2)}) %copy-start.3) | copy-done | bytes 16408
  5.5 0.0 copy-start.4
  5.5 0.7 %copy-done.4 = f32[16,256]{1,0:T(8,128)S(1)} copy-done((f32[16,256]{1,0:T(8,128)S(1)}, f32[16,256]{1,0:T(8,128)}, u32[]{:S(2)}) %copy-start.4) | copy-done | bytes 16408
  6.3 1.0 %fields.1.refs_2_ = f32[2,32,128]{2,1,0:T(8,128)S(1)} custom-call(s32[16]{0:T(128)S(1)} %copy-done.5, s32[16,256]{1,0:T(8,128)S(1)} %copy-done.2, f32[16,256]{1,0:T(8,128)S(1)} %copy-done.3, f32[16,256]{1,0:T(8,128)S(1)} %copy-done.4), custom_call_target="tpu_custom_call" | custom-call | tf_op jit(solution)/shard_map/fields/pallas_call | solution.py:326
  7.3 0.1 collective-permute-done.radius_ref
  7.4 0.9 %collective-permute-done.1.refs_1_ = bf16[32,32,128]{2,1,0:T(8,128)(2,1)S(1)} collective-permute-done((bf16[32,32,128]{2,1,0:T(8,128)(2,1)}, bf16[32,32,128]{2,1,0:T(8,128)(2,1)S(1)}, u32[]{:S(2)}, u32[]{:S(2)}) %collective-permute-start.1) | collective-permute-done | bytes 262176 | tf_op jit(solution)/shard_map/ppermute | solution.py:324
  8.3 0.0 copy-start.1
  8.3 0.9 %copy-done.1 = bf16[32,32,128]{2,1,0:T(8,128)(2,1)S(1)} copy-done((bf16[32,32,128]{2,1,0:T(8,128)(2,1)S(1)}, bf16[32,32,128]{2,1,0:T(8,128)(2,1)}, u32[]{:S(2)}) %copy-start.1) | copy-done | bytes 262168
  9.2 2.1 %outward_gram.1 = (bf16[8,64,128]{2,1,0:T(8,128)(2,1)S(1)}, bf16[16,64,128]{2,1,0:T(8,128)(2,1)S(1)}, f32[2,32,128]{2,1,0:T(8,128)S(1)}, bf16[528,128]{1,0:T(8,128)(2,1)S(1)}) custom-call(s32[2]{0:T(128)S(1)} %pad_add_fusion.place_ref, s32[16]{0:T(128)S(1)} %collective-permute-done.radius_ref, bf16[32,32,128]{2,1,0:T(8,128)(2,1)S(1)} %copy-done.1, ...), custom_call_target="tpu_custom_call" | custom-call | tf_op jit(solution)/shard_map/outward_gram/pallas_call | solution.py:340
  11.4 3.6 %collective-permute-start.2 = (bf16[528,128]{1,0:T(8,128)(2,1)S(1)}, bf16[528,128]{1,0:T(8,128)(2,1)S(1)}, u32[]{:S(2)}, u32[]{:S(2)}) collective-permute-start(bf16[528,128]{1,0:T(8,128)(2,1)S(1)} %get-tuple-element.16), channel_id=1, source_target_pairs={{2,0},{4,2},{6,4},{8,6},{10,8},{12,10},{14,12},{16,14},{18,16},{20... | collective-permute-start | bytes 405512 | tf_op jit(solution)/shard_map/ppermute | solution.py:355
  15.0 0.0 copy-start.6
  15.0 0.6 %copy-done.6 = s32[16]{0:T(128)S(1)} copy-done((s32[16]{0:T(128)S(1)}, s32[16]{0:T(128)}, u32[]{:S(2)}) %copy-start.6) | copy-done | bytes 88
  15.6 0.0 copy-start
  15.6 1.9 %own_gram.1.own_ref = f32[520,128]{1,0:T(8,128)S(1)} custom-call(s32[2]{0:T(128)S(1)} %pad_add_fusion.place_ref, s32[16]{0:T(128)S(1)} %copy-done.6, bf16[8,64,128]{2,1,0:T(8,128)(2,1)S(1)} %get-tuple-element.13.near_ref, bf16[16,64,128]{2,1,0:T(8,128)(2,1)S(1)} %get-tuple-element.14.far_ref, f32[2,32,128]{2,1,0:T(8,128)S(1)} %get-tuple-element.15.field_ref.after_ref), custom_call_target="tpu_custom_call" | custom-call | tf_op jit(solution)/shard_map/own_gram/pallas_call | solution.py:356
  17.5 0.0 collective-permute-done.2.message_ref
  17.6 2.6 %collective-permute-start.3 = (bf16[528,128]{1,0:T(8,128)(2,1)S(1)}, bf16[528,128]{1,0:T(8,128)(2,1)S(1)}, u32[]{:S(2)}, u32[]{:S(2)}) collective-permute-start(bf16[528,128]{1,0:T(8,128)(2,1)S(1)} %get-tuple-element.18), channel_id=1, source_target_pairs={{0,1},{1,0},{2,3},{3,2},{4,5},{5,4},{6,7},{7,6},{8,9},{9,8},{10,11... | collective-permute-start | bytes 405512 | tf_op jit(solution)/shard_map/ppermute | solution.py:382
  20.2 0.0 copy-done
  20.2 0.8 %state.1 = (bf16[32,64,128]{2,1,0:T(8,128)(2,1)S(1)}, f32[32,128]{1,0:T(8,128)S(1)}) custom-call(f32[2,32,128]{2,1,0:T(8,128)S(1)} %get-tuple-element.15.field_ref.after_ref, bf16[64,32,128]{2,1,0:T(8,128)(2,1)S(1)} %bitcast.2), custom_call_target="tpu_custom_call" | custom-call | tf_op jit(solution)/shard_map/state/pallas_call | solution.py:362
  21.0 3.0 %collective-permute-done.3.other_ref = bf16[528,128]{1,0:T(8,128)(2,1)S(1)} collective-permute-done((bf16[528,128]{1,0:T(8,128)(2,1)S(1)}, bf16[528,128]{1,0:T(8,128)(2,1)S(1)}, u32[]{:S(2)}, u32[]{:S(2)}) %collective-permute-start.3) | collective-permute-done | bytes 135200 | tf_op jit(solution)/shard_map/ppermute | solution.py:382
  24.0 4.7 %finish.1 = bf16[1,64,32,128]{3,2,1,0:T(8,128)(2,1)} custom-call(f32[520,128]{1,0:T(8,128)S(1)} %get-tuple-element.17.total_ref, bf16[528,128]{1,0:T(8,128)(2,1)S(1)} %collective-permute-done.3.other_ref, bf16[32,64,128]{2,1,0:T(8,128)(2,1)S(1)} %get-tuple-element.19.lag_ref, f32[32,128]{1,0:T(8,128)S(1)} %get-tuple-element.20.mean_ref), custom_call_target="tpu_custom_call" | custom-call | tf_op jit(solution)/shard_map/finish/pallas_call | solution.py:383
  (1 shorter events, 0.0 us)
Async XLA Ops:
  0.0 8.3 %collective-permute-start.1 = (bf16[32,32,128]{2,1,0:T(8,128)(2,1)}, bf16[32,32,128]{2,1,0:T(8,128)(2,1)S(1)}, u32[]{:S(2)}, u32[]{:S(2)}) collective-permute-start(bf16[32,32,128]{2,1,0:T(8,128)(2,1)} %refs_0_.1), channel_id=1, source_target_pairs={{1,0},{0,1},{3,2},{2,3},{5,4},{4,5},{7,6},{6,7},{9,8},{8,9},{11,10... | collective-permute-start | bytes 786440 | tf_op jit(solution)/shard_map/ppermute | solution.py:324
  1.5 5.9 %collective-permute-start = (s32[16]{0:T(128)}, s32[16]{0:T(128)S(1)}, u32[]{:S(2)}, u32[]{:S(2)}) collective-permute-start(s32[16]{0:T(128)} %radius_ref.1), channel_id=1, source_target_pairs={{0,2},{2,4},{4,6},{6,8},{8,10},{10,12},{12,14},{14,16},{16,18},{18... | collective-permute-start | bytes 200 | tf_op jit(solution)/shard_map/ppermute | solution.py:325
  3.4 0.7 %copy-start.5 = (s32[16]{0:T(128)S(1)}, s32[16]{0:T(128)}, u32[]{:S(2)}) copy-start(s32[16]{0:T(128)} %alive_hbm.1) | copy-start | bytes 196
  4.1 0.7 %copy-start.2 = (s32[16,256]{1,0:T(8,128)S(1)}, s32[16,256]{1,0:T(8,128)}, u32[]{:S(2)}) copy-start(s32[16,256]{1,0:T(8,128)} %spot_hbm.1) | copy-start | bytes 49156
  4.8 0.7 %copy-start.3 = (f32[16,256]{1,0:T(8,128)S(1)}, f32[16,256]{1,0:T(8,128)}, u32[]{:S(2)}) copy-start(f32[16,256]{1,0:T(8,128)} %level_hbm.1) | copy-start | bytes 49156
  5.5 0.7 %copy-start.4 = (f32[16,256]{1,0:T(8,128)S(1)}, f32[16,256]{1,0:T(8,128)}, u32[]{:S(2)}) copy-start(f32[16,256]{1,0:T(8,128)} %prec_hbm.1) | copy-start | bytes 49156
  8.3 1.0 %copy-start.1 = (bf16[32,32,128]{2,1,0:T(8,128)(2,1)S(1)}, bf16[32,32,128]{2,1,0:T(8,128)(2,1)}, u32[]{:S(2)}) copy-start(bf16[32,32,128]{2,1,0:T(8,128)(2,1)} %refs_0_.1) | copy-start | bytes 786436
  11.4 6.2 %collective-permute-start.2 = (bf16[528,128]{1,0:T(8,128)(2,1)S(1)}, bf16[528,128]{1,0:T(8,128)(2,1)S(1)}, u32[]{:S(2)}, u32[]{:S(2)}) collective-permute-start(bf16[528,128]{1,0:T(8,128)(2,1)S(1)} %get-tuple-element.16), channel_id=1, source_target_pairs={{2,0},{4,2},{6,4},{8,6},{10,8},{12,10},{14,12},{16,14},{18,16},{20... | collective-permute-start | bytes 405512 | tf_op jit(solution)/shard_map/ppermute | solution.py:355
  15.0 0.7 %copy-start.6 = (s32[16]{0:T(128)S(1)}, s32[16]{0:T(128)}, u32[]{:S(2)}) copy-start(s32[16]{0:T(128)} %radius_ref.1) | copy-start | bytes 196
  15.6 4.6 %copy-start = (bf16[1,64,32,128]{3,2,1,0:T(8,128)(2,1)S(1)}, bf16[1,64,32,128]{3,2,1,0:T(8,128)(2,1)}, u32[]{:S(2)}) copy-start(bf16[1,64,32,128]{3,2,1,0:T(8,128)(2,1)} %param.7) | copy-start | bytes 1572868
  17.6 6.4 %collective-permute-start.3 = (bf16[528,128]{1,0:T(8,128)(2,1)S(1)}, bf16[528,128]{1,0:T(8,128)(2,1)S(1)}, u32[]{:S(2)}, u32[]{:S(2)}) collective-permute-start(bf16[528,128]{1,0:T(8,128)(2,1)S(1)} %get-tuple-element.18), channel_id=1, source_target_pairs={{0,1},{1,0},{2,3},{3,2},{4,5},{5,4},{6,7},{7,6},{8,9},{9,8},{10,11... | collective-permute-start | bytes 405512 | tf_op jit(solution)/shard_map/ppermute | solution.py:382
